TPU v7x, 256 devices: a whole 4x4x8 slice. The times are simulated.
256 devices in a mesh: tile: 64 (over y, z, core), sub: 4 (over x).
Axes of the slice: x: 4, y: 4, z: 8, core: 2. Of those that a mesh axis runs over, the one named last changes fastest.
Arguments:
- condition: bfloat16 [12, 16384, 1024], P(None, 'tile', 'sub'), may hold values from -6 to 6
- state: float32 [4, 16384, 1024], P(None, 'tile', 'sub'), may hold values from -12 to 12
- corner_rows: int32 [64, 4, 2], P('tile', 'sub'), may hold values from 0 to 256
- corner_cols: int32 [64, 4, 2], P('tile', 'sub'), may hold values from 0 to 256
- live_counts: int32 [64, 4], P('tile', 'sub'), may hold values from 1 to 2, as said below
- blend_weight: float32 [64, 4, 2, 128, 128], P('tile', 'sub'), may hold values from 0.2 to 5
- conv_in: bfloat16 [3, 3, 64, 16], replicated, may hold values from -0.5 to 0.5
- conv_mid: bfloat16 [3, 3, 64, 64], replicated, may hold values from -0.25 to 0.25
- proj_out: bfloat16 [4, 64], replicated, may hold values from -0.75 to 0.75
Outputs:
- denoised: float32 [4, 16384, 1024], P(None, 'tile', 'sub')
- next_state: float32 [4, 16384, 1024], P(None, 'tile', 'sub')
Inputs may be any that keep to these rules, and one draw needn't show every extreme that they name: `live_counts`: each device has at least one and at most 2 live patches; some device has exactly 2.
All inputs are finite; a program needn't handle non-finite values.
Results may differ from a plain program's by a relative error of at most 0.00085.
Values may be sent and summed in bfloat16 or wider, within the bound.
No kernel may reach another device: no remote copies, remote signals or barrier semaphores. Data moves between devices by JAX's collectives and lax.ppermute only.
A program may use at most 128 MiB of HBM per device.

v0:
```python
import jax
import jax.numpy as jnp
from jax import lax
from jax.experimental import pallas as pl
from jax.experimental.pallas import tpu as pltpu
from jax.sharding import PartitionSpec as P

SIGMA = 2.0
SIGMA_NEXT = 1.6
C_IN = 1.0 / (SIGMA * SIGMA + 0.25) ** 0.5
C_SKIP = 0.25 / (SIGMA * SIGMA + 0.25)
C_OUT = 0.5 * SIGMA / (SIGMA * SIGMA + 0.25) ** 0.5

BY = 256
BX = 256
SIDE = 128
HALF = 64
CC = 12
CH = 16
HID = 64
OUT = 4
SLOTS = 2
LANES = 128
WIDE = 2 * LANES
STEP = 8
X_TOP = 10
X_ROWS = BY + 24
ACC_ROWS = BY + 2 * STEP
LAG = 3
UNITS = 768
PIECES = 9 * SLOTS
TILE_MSG = 2 * HALF + 4 * CH + 16
SUB_MSG = SIDE + 2 * HALF + 4 * CH + 64 + 16
F32 = jnp.float32
BF16 = jnp.bfloat16


def iota(shape, dim):
    return lax.broadcasted_iota(jnp.int32, shape, dim)


def scaled(state):
    return (state * C_IN).astype(BF16)


def own_meta(rows_ref, cols_ref, live_ref):
    sub = iota((16, LANES), 0)
    values = (rows_ref[0, 0, 0], rows_ref[0, 0, 1], cols_ref[0, 0, 0], cols_ref[0, 0, 1], live_ref[0, 0])
    tile = jnp.zeros((16, LANES), jnp.int32)
    for k, value in enumerate(values):
        tile = jnp.where(sub == k, value, tile)
    return tile


def pack_tile(rows_ref, cols_ref, live_ref, c_top, c_bot, s_top, s_bot, weight_ref, up_ref, down_ref, tmp):
    meta = own_meta(rows_ref, cols_ref, live_ref).astype(F32).astype(BF16)
    for out, cond, state, low, first_c, first_s in (
        (up_ref, c_top, s_top, 0, 0, 0),
        (down_ref, c_bot, s_bot, HALF, 14, 6),
    ):
        for p in range(SLOTS):
            out[p * HALF : (p + 1) * HALF, :] = weight_ref[0, 0, p, low : low + HALF, :].astype(BF16)
        for c in range(CH):
            if c < CC:
                tile = cond[c].astype(F32)[first_c : first_c + 2, :]
            else:
                tile = scaled(state[c - CC]).astype(F32)[first_s : first_s + 2, :]
            for t in range(2):
                for r in range(2):
                    at = t * 2 * CH + r * CH + c
                    tmp[at : at + 1, :] = tile[r : r + 1, t * LANES : (t + 1) * LANES]
        out[2 * HALF : 2 * HALF + 4 * CH, :] = tmp[...].astype(BF16)
        out[2 * HALF + 4 * CH :, :] = meta


def prepare(cond_ref, state_ref, body_ref, edge_ref):
    to = iota((CH * CH, CH * CH), 0)
    of = iota((CH * CH, CH * CH), 1)
    turn = (of == (to % CH) * CH + to // CH).astype(F32).astype(BF16)
    picks = iota((16, LANES), 0)
    spots = iota((16, LANES), 1)
    first = ((picks == spots) & (picks < 2)).astype(F32).astype(BF16)
    last = ((picks == spots - (LANES - 4)) & (picks >= 2)).astype(F32).astype(BF16)

    def group(i, carry):
        for e in range(4):
            start = pl.multiple_of((4 * i + e) * CH, CH)
            rows = pl.ds(start, CH)
            value = jnp.concatenate(
                [cond_ref[:, rows, :].reshape(CC * CH, BX), scaled(state_ref[:, rows, :]).reshape(OUT * CH, BX)], axis=0
            )
            value = jnp.dot(turn, value, preferred_element_type=F32).astype(BF16)
            at = pl.ds(start * CH, CH * CH)
            edge = jnp.zeros((16, CH * CH), F32)
            for t, pick in enumerate((first, last)):
                part = value[:, t * LANES : (t + 1) * LANES]
                body_ref[t, at, :] = part
                edge = edge + lax.dot_general(pick, part, (((1,), (1,)), ((), ())), preferred_element_type=F32)
            edge_ref[:, at] = edge.astype(BF16)
        return carry

    lax.fori_loop(0, BY // CH // 4, group, 0)


def pack_sub(rows_ref, cols_ref, live_ref, weight_ref, edge_ref, above_ref, below_ref, left_ref, right_ref):
    lane = iota((1, LANES), 1)
    meta0 = own_meta(rows_ref, cols_ref, live_ref).astype(F32)
    sub = iota((16, LANES), 0)
    first = 2 * HALF + 4 * CH
    meta_a = pltpu.roll(above_ref[first:, :].astype(F32), 5, 0)
    meta_b = pltpu.roll(below_ref[first:, :].astype(F32), 10, 0)
    meta = jnp.where(sub < 5, meta0, jnp.where(sub < 10, meta_a, meta_b)).astype(BF16)
    for out, side in ((left_ref, 0), (right_ref, 1)):
        def packed(one, two):
            if side == 0:
                return jnp.where(lane < HALF, one, pltpu.roll(two, HALF, 1)).astype(BF16)
            return jnp.where(lane < HALF, pltpu.roll(one, HALF, 1), two).astype(BF16)

        out[0:SIDE, :] = packed(weight_ref[0, 0, 0], weight_ref[0, 0, 1])
        at = SIDE
        for msg in (above_ref, below_ref):
            out[at : at + HALF, :] = packed(msg[0:HALF, :].astype(F32), msg[HALF : 2 * HALF, :].astype(F32))
            at += HALF
        for msg in (above_ref, below_ref):
            begin = 2 * HALF + side * 2 * CH
            out[at : at + 2 * CH, :] = msg[begin : begin + 2 * CH, :]
            at += 2 * CH
        edge = edge_ref[...].astype(F32)
        for m in range(4):
            rows = []
            for e in range(8):
                spot = (8 * m + e) * LANES
                rows.append(edge[2 * side : 2 * side + 2, spot : spot + LANES])
            out[at : at + 16, :] = jnp.concatenate(rows, axis=0).astype(BF16)
            at += 16
        out[at:, :] = meta


def main_kernel(
    rows_ref, cols_ref, live_ref, body_ref, state_ref, weight_ref,
    above_ref, below_ref, left_ref, right_ref, w1_ref, w2_ref, w3_ref,
    den_ref, next_ref,
    xb_ref, p_ref, a_ref, u_ref, q_ref, acc_ref, wall_ref, meta_v, meta_s, unit_ref, place_ref, list_ref, sem, body_sem,
):
    lane = iota((1, LANES), 1)
    first = 2 * HALF + 4 * CH
    meta_v[0:16, :] = own_meta(rows_ref, cols_ref, live_ref)
    meta_v[16:32, :] = above_ref[first:, :].astype(F32).astype(jnp.int32)
    meta_v[32:48, :] = below_ref[first:, :].astype(F32).astype(jnp.int32)
    meta_v[48:64, :] = left_ref[SUB_MSG - 16 :, :].astype(F32).astype(jnp.int32)
    meta_v[64:80, :] = right_ref[SUB_MSG - 16 :, :].astype(F32).astype(jnp.int32)
    copy = pltpu.make_async_copy(meta_v, meta_s, sem)
    copy.start()

    body = pltpu.make_async_copy(body_ref, xb_ref.at[1:3, X_TOP * CH : (BY + X_TOP) * CH, :], body_sem)
    body.start()
    corner = SIDE + 2 * HALF
    for msg, row, spot in ((above_ref, X_TOP - 2, 0), (below_ref, BY + X_TOP, 2 * CH)):
        for t in range(2):
            xb_ref[t + 1, row * CH : (row + 2) * CH, :] = msg[2 * HALF + t * 2 * CH : 2 * HALF + (t + 1) * 2 * CH, :]
        from_left = left_ref[corner + spot : corner + spot + 2 * CH, :].astype(F32)
        from_right = right_ref[corner + spot : corner + spot + 2 * CH, :].astype(F32)
        xb_ref[0, row * CH : (row + 2) * CH, :] = jnp.where(
            lane < 2, from_right, jnp.where(lane >= LANES - 2, from_left, 0.0)
        ).astype(BF16)
    edge_at = corner + 4 * CH
    picks = iota((32, LANES), 0)
    spots = iota((32, LANES), 1)
    for m in range(4):
        rows = slice(edge_at + 16 * m, edge_at + 16 * m + 16)
        both = jnp.concatenate([left_ref[rows, :].astype(F32), right_ref[rows, :].astype(F32)], axis=0)
        turned = both.T.astype(BF16)
        for e in range(8):
            to_left = (picks - 2 * e == spots - (LANES - 2)) & (spots >= LANES - 2) & (picks < 16)
            to_right = (picks - 16 - 2 * e == spots) & (spots < 2) & (picks >= 16)
            place = (to_left | to_right).astype(F32).astype(BF16)
            at = X_TOP * CH + (8 * m + e) * LANES
            xb_ref[0, at : at + LANES, :] = jnp.dot(turned, place, preferred_element_type=F32).astype(BF16)
    for t in range(3):
        xb_ref[t, 0 : (X_TOP - 2) * CH, :] = jnp.zeros(((X_TOP - 2) * CH, LANES), BF16)
        low = (BY + X_TOP + 2) * CH
        xb_ref[t, low:, :] = jnp.zeros((X_ROWS * CH - low, LANES), BF16)
    p_ref[...] = jnp.zeros_like(p_ref)
    a_ref[...] = jnp.zeros_like(a_ref)

    for p in range(SLOTS):
        wall_ref[p, 0:SIDE, :] = weight_ref[0, 0, p]
        wall_ref[2 + p, HALF:SIDE, :] = above_ref[p * HALF : (p + 1) * HALF, :].astype(F32)
        wall_ref[4 + p, 0:HALF, :] = below_ref[p * HALF : (p + 1) * HALF, :].astype(F32)
        for d, msg in ((3, left_ref), (6, right_ref)):
            def side(lo, hi):
                part = msg[lo:hi, :].astype(F32)
                return jnp.where((lane < HALF) == (p == 0), part, pltpu.roll(part, HALF, 1))

            wall_ref[2 * d + p, 0:SIDE, :] = side(0, SIDE)
            wall_ref[2 * d + 2 + p, HALF:SIDE, :] = side(SIDE, SIDE + HALF)
            wall_ref[2 * d + 4 + p, 0:HALF, :] = side(SIDE + HALF, SIDE + 2 * HALF)

    def clear(i, carry):
        for t in range(1, 3):
            acc_ref[t, pl.ds(pl.multiple_of(i * 256 + STEP * 8, 64), 256), :] = jnp.zeros((256, LANES), F32)
        return carry

    lax.fori_loop(0, BY * 8 // 256, clear, 0)
    copy.wait()

    one_row = (iota((8, 1), 0) == OUT).astype(F32)

    def nothing(i):
        unit_ref[0, i] = 0
        unit_ref[1, i] = 0
        unit_ref[2, i] = BY
        unit_ref[3, i] = 0

    for i in range(4 * LAG):
        nothing(i)

    pos = jnp.int32(0)
    totals = []
    pieces = []
    for k in range(PIECES):
        d, p = k // 2, k % 2
        across, along = d // 3, d % 3
        base = 16 * along if across == 0 else 32 + 16 * across + 5 * along
        row0 = meta_s[base + p, 0] + (0, -BY, BY)[along] - HALF
        col0 = meta_s[base + 2 + p, 0] + (0, -BX, BX)[across] - HALF
        low = jnp.maximum(-row0, 0) // STEP
        high = (jnp.minimum(SIDE, BY - row0) + STEP - 1) // STEP
        touches = (low < high) & (col0 > -SIDE) & (col0 < BX) & (p < meta_s[base + 4, 0])
        spot = col0 + LANES
        q, rem = spot // LANES, spot % LANES
        after_q = jnp.where(q == 2, 0, q + 1)
        whole = ((q, rem, q, rem, LANES), (after_q, rem, after_q, 0, rem))
        bound = LANES - rem
        if across == 0:
            narrow = jnp.bool_(False)
        else:
            if across == 1:
                narrow = spot <= HALF - 2
                ours = [(3, (spot + HALF * (1 - g)) % LANES, 1, 0, spot) for g in range(2)]
            else:
                narrow = col0 >= BX - (HALF - 2)
                ours = [(4, (spot + HALF * g) % LANES, 2, col0 - LANES, LANES) for g in range(2)]
            whole = [[jnp.where(narrow, x, y) for x, y in zip(mine, all_)] for mine, all_ in zip(ours, whole)]
            bound = jnp.where(narrow, HALF, bound)
        for g in range(2):
            for f in range(5):
                place_ref[5 * g + f, k] = whole[g][f]
        place_ref[10, k] = bound
        pieces.append((k, low, high, row0, touches, narrow))
    for half in range(2):
        total = jnp.int32(0)
        for k, low, high, row0, touches, narrow in pieces:
            if half == 1 and k < 6:
                continue
            ours = touches & (narrow if half == 1 else jnp.logical_not(narrow))
            list_ref[0, pos] = k
            list_ref[1, pos] = low
            list_ref[2, pos] = high
            list_ref[3, pos] = row0
            list_ref[4, pos] = half
            pos = pos + ours.astype(jnp.int32)
            total = total + jnp.where(ours, high - low, 0)
        totals.append(total)
    for i in range(8 * LAG + 16):
        list_ref[0, pos + i] = 0
        list_ref[1, pos + i] = 0
        list_ref[2, pos + i] = 1
        list_ref[3, pos + i] = BY
        list_ref[4, pos + i] = 1
    count = totals[0] + (totals[1] + 1) // 2 + 2 * LAG
    body.wait()

    def edges(i, carry):
        at = pl.ds(pl.multiple_of(i * (X_ROWS * CH // 5), CH), X_ROWS * CH // 5)
        outer = xb_ref[0, at, :]
        xb_ref[3, at, :] = jnp.where(lane < HALF, xb_ref[1, at, :], outer)
        xb_ref[4, at, :] = jnp.where(lane < HALF, outer, xb_ref[2, at, :])
        return carry

    lax.fori_loop(0, 5, edges, 0)

    def advance(unit, g, at, i):
        half = list_ref[4, at]
        unit_ref[0, unit] = list_ref[0, at]
        unit_ref[1, unit] = i * STEP
        unit_ref[2, unit] = list_ref[3, at] + i * STEP
        unit_ref[3, unit] = half
        ahead = i + (half if g == 0 else 1)
        done = ahead >= list_ref[2, at]
        at = at + done.astype(jnp.int32)
        return at, jnp.where(done, list_ref[1, at], ahead)

    first_half = lane < HALF

    def by_half(values):
        return jnp.where(first_half, values[0].astype(F32), values[1].astype(F32))

    def borders(split):
        lo = jnp.where((lane == 0) | ((lane == HALF) & (split > 0)), 0.0, 1.0)
        hi = jnp.where((lane == LANES - 1) | ((lane == HALF - 1) & (split > 0)), 0.0, 1.0)
        return [jnp.broadcast_to(part, (CH, LANES)).astype(BF16) for part in (lo, hi)]

    def keep(ref, z, row, h, part, mask):
        for m in range(part.shape[0] // CH):
            ref[z, row + m * CH : row + (m + 1) * CH, h * LANES : (h + 1) * LANES] = jnp.where(mask > 0, part[m * CH : (m + 1) * CH], jnp.zeros((), BF16))

    def blend(i):
        nets = [
            jnp.dot(w3_ref[...], q_ref[4 * e * HID : 4 * (e + 1) * HID, :], preferred_element_type=F32)
            for e in range(STEP // 4)
        ]
        for h in range(2):
            units = [4 * i + 2 * h + g for g in range(2)]
            ks = [unit_ref[0, unit] for unit in units]
            locals_ = [unit_ref[1, unit] for unit in units]
            parts = []
            for f in range(STEP):
                y = nets[f // 4][8 * (f % 4) : 8 * (f % 4) + 8, h * LANES : (h + 1) * LANES]
                one, two = [wall_ref[k, pl.ds(local + f, 1), :] for k, local in zip(ks, locals_)]
                parts.append((y + one_row) * jnp.where(first_half, one, two))
            value = jnp.concatenate(parts, axis=0)
            for g in range(2):
                turn, tile, lo, hi = [place_ref[5 * g + f, ks[g]] for f in range(1, 5)]
                y = pltpu.roll(value, turn, 1)
                at = pl.ds(pl.multiple_of((unit_ref[2, units[g]] + STEP) * 8, 8), 8 * STEP)
                acc_ref[tile, at, :] += jnp.where((lane >= lo) & (lane < hi), y, 0.0)

    def second_conv(z):
        for e in range(STEP // 2):
            v = jnp.dot(w2_ref[...], a_ref[z, 2 * e * 3 * HID : (2 * e + 4) * 3 * HID, :], preferred_element_type=F32)
            v = v + u_ref[z, (2 * e + 1) * HID : (2 * e + 3) * HID, :]
            q_ref[2 * e * HID : (2 * e + 2) * HID, :] = (v + v * jnp.tanh(v)).astype(BF16)

    def first_conv(i, z):
        for e in range(STEP // 2 + 1):
            u = jnp.dot(w1_ref[...], p_ref[z, 2 * e * 3 * CH : (2 * e + 4) * 3 * CH, :], preferred_element_type=F32)
            u_ref[z, 2 * e * HID : (2 * e + 2) * HID, :] = u
            act = u + u * jnp.tanh(u)
            for h in range(2):
                units = [4 * i + 2 * h + g for g in range(2)]
                locals_ = [unit_ref[1, unit] for unit in units]
                inner_lo, inner_hi = borders(unit_ref[3, units[0]])
                for r in range(2):
                    mid = act[r * HID : (r + 1) * HID, h * LANES : (h + 1) * LANES]
                    row = 2 * e + r
                    if row == 0:
                        mid = mid * by_half([local > 0 for local in locals_])
                    if row == STEP + 1:
                        mid = mid * by_half([local < SIDE - STEP for local in locals_])
                    mid = mid.astype(BF16)
                    at = row * 3 * HID
                    keep(a_ref, z, at, h, pltpu.roll(mid, 1, 1), inner_lo)
                    a_ref[z, at + HID : at + 2 * HID, h * LANES : (h + 1) * LANES] = mid
                    keep(a_ref, z, at + 2 * HID, h, pltpu.roll(mid, LANES - 1, 1), inner_hi)

    def stage(i, z):
        for h in range(2):
            units = [4 * i + 2 * h + g for g in range(2)]
            locals_ = [unit_ref[1, unit] for unit in units]
            inner_lo, inner_hi = borders(unit_ref[3, units[0]])
            ks = [unit_ref[0, unit] for unit in units]
            tiles = [place_ref[5 * g, ks[g]] for g in range(2)]
            turns = [(LANES - place_ref[5 * g + 1, ks[g]]) % LANES for g in range(2)]
            rows = [unit_ref[2, unit] for unit in units]
            low_part = lane < place_ref[10, ks[0]]
            both = []
            for tile, turn, row in zip(tiles, turns, rows):
                at = pl.ds(pl.multiple_of((row + X_TOP - 2) * CH, CH), (STEP + 4) * CH)
                both.append(pltpu.roll(xb_ref[tile, at, :], turn, 1))
            value = jnp.where(low_part, both[0], both[1])
            for j in range(STEP + 4):
                mid = value[j * CH : (j + 1) * CH]
                if j < 2:
                    mid = mid * by_half([local > 0 for local in locals_]).astype(BF16)
                if j >= STEP + 2:
                    mid = mid * by_half([local < SIDE - STEP for local in locals_]).astype(BF16)
                keep(p_ref, z, j * 3 * CH, h, pltpu.roll(mid, 1, 1), inner_lo)
                p_ref[z, j * 3 * CH + CH : j * 3 * CH + 2 * CH, h * LANES : (h + 1) * LANES] = mid
                keep(p_ref, z, j * 3 * CH + 2 * CH, h, pltpu.roll(mid, LANES - 1, 1), inner_hi)

    def step(i, carry):
        at, row = carry
        for z in range(2):
            blend(2 * i + z)
            first_conv(2 * i + z + 2, z)
            second_conv(1 - z)
            stage(2 * i + z + 3, 1 - z)
        return more(i + 1, at, row)

    def more(i, at, row):
        for h in range(8):
            at, row = advance(8 * i + 4 * LAG + h, h % 2, at, row)
        return at, row

    lax.fori_loop(0, (count + 3) // 4, step, more(0, jnp.int32(0), list_ref[1, 0]))

    def finish(i, carry):
        for t, part in ((t, part) for part in range(4) for t in range(2)):
            row = pl.multiple_of(i * 32 + part * 8, 8)
            lanes = slice(t * LANES, (t + 1) * LANES)
            total = acc_ref[t + 1, pl.ds((row + STEP) * 8 + OUT, 8, stride=8), :]
            over = 1.0 / (1.0 + total)
            for o in range(OUT):
                state = state_ref[o, pl.ds(row, 8), lanes]
                numer = acc_ref[t + 1, pl.ds((row + STEP) * 8 + o, 8, stride=8), :]
                den = (state * (1.0 + C_SKIP * total) + C_OUT * numer) * over
                den_ref[o, pl.ds(row, 8), lanes] = den
                next_ref[o, pl.ds(row, 8), lanes] = state + (SIGMA_NEXT - SIGMA) * (state - den) / SIGMA
        return carry

    lax.fori_loop(0, BY // 32, finish, 0)


def banded(kernel, times):
    outs, chans = kernel.shape[2], kernel.shape[3]
    flat = (0.5 * jnp.transpose(kernel, (2, 0, 1, 3))).astype(BF16).reshape(outs, 9 * chans)
    step = 3 * chans
    return jnp.concatenate([jnp.pad(flat, ((0, 0), (r * step, (times - 1 - r) * step))) for r in range(times)], axis=0)


def shifted(value, axis, steps):
    count = lax.axis_size(axis)
    first, last = max(0, -steps), min(count, count - steps)
    return lax.ppermute(value, axis, [(i, i + steps) for i in range(first, last)])


def per_device(condition, state, corner_rows, corner_cols, live_counts, blend_weight, conv_in, conv_mid, proj_out):
    smem = pl.BlockSpec(memory_space=pltpu.SMEM)
    vmem = pl.BlockSpec(memory_space=pltpu.VMEM)
    whole_w = pl.BlockSpec((1, 1, SLOTS, SIDE, SIDE), lambda i: (0, 0, 0, 0, 0))
    msg = jax.ShapeDtypeStruct((TILE_MSG, LANES), BF16)
    up, down = pl.pallas_call(
        pack_tile,
        grid=(1,),
        in_specs=[
            smem, smem, smem,
            pl.BlockSpec((CC, 16, BX), lambda i: (0, 0, 0)),
            pl.BlockSpec((CC, 16, BX), lambda i: (0, BY // 16 - 1, 0)),
            pl.BlockSpec((OUT, 8, BX), lambda i: (0, 0, 0)),
            pl.BlockSpec((OUT, 8, BX), lambda i: (0, BY // 8 - 1, 0)),
            whole_w,
        ],
        out_specs=[pl.BlockSpec((TILE_MSG, LANES), lambda i: (0, 0))] * 2,
        out_shape=[msg, msg],
        scratch_shapes=[pltpu.VMEM((4 * CH, LANES), F32)],
        name="pack_tile",
    )(corner_rows, corner_cols, live_counts, condition, condition, state, state, blend_weight)
    above = shifted(down, "tile", 1)
    below = shifted(up, "tile", -1)
    w1 = banded(conv_in, 2)
    w2 = banded(conv_mid, 2)
    rows8 = jnp.pad(proj_out, ((0, 8 - OUT), (0, 0)))
    w3 = jnp.concatenate([jnp.pad(rows8, ((0, 0), (r * HID, (3 - r) * HID))) for r in range(4)], axis=0)
    body, edge = pl.pallas_call(
        prepare,
        in_specs=[vmem] * 2,
        out_specs=[vmem] * 2,
        out_shape=[jax.ShapeDtypeStruct((2, BY * CH, LANES), BF16), jax.ShapeDtypeStruct((16, BY * CH), BF16)],
        name="prepare",
        compiler_params=pltpu.CompilerParams(vmem_limit_bytes=16 << 20),
        cost_estimate=pl.CostEstimate(flops=2 * 4096 * 256 * 256, bytes_accessed=5 << 20, transcendentals=0),
    )(condition, state)
    msg = jax.ShapeDtypeStruct((SUB_MSG, LANES), BF16)
    left, right = pl.pallas_call(
        pack_sub,
        in_specs=[smem] * 3 + [vmem] * 4,
        out_specs=[vmem] * 2,
        out_shape=[msg, msg],
        name="pack_sub",
        compiler_params=pltpu.CompilerParams(vmem_limit_bytes=16 << 20),
    )(corner_rows, corner_cols, live_counts, blend_weight, edge, above, below)
    from_left = shifted(right, "sub", 1)
    from_right = shifted(left, "sub", -1)
    out = jax.ShapeDtypeStruct((OUT, BY, BX), F32)
    return tuple(pl.pallas_call(
        main_kernel,
        in_specs=[smem] * 3 + [vmem] * 10,
        out_specs=[vmem] * 2,
        out_shape=[out, out],
        scratch_shapes=[
            pltpu.VMEM((5, X_ROWS * CH, LANES), BF16),
            pltpu.VMEM((2, (STEP + 4) * 3 * CH, WIDE), BF16),
            pltpu.VMEM((2, (STEP + 2) * 3 * HID, WIDE), BF16),
            pltpu.VMEM((2, (STEP + 2) * HID, WIDE), F32),
            pltpu.VMEM((STEP * HID, WIDE), BF16),
            pltpu.VMEM((3, ACC_ROWS * 8, LANES), F32),
            pltpu.VMEM((PIECES, SIDE, LANES), F32),
            pltpu.VMEM((80, LANES), jnp.int32),
            pltpu.SMEM((80, LANES), jnp.int32),
            pltpu.SMEM((4, UNITS), jnp.int32),
            pltpu.SMEM((11, PIECES), jnp.int32),
            pltpu.SMEM((5, LANES), jnp.int32),
            pltpu.SemaphoreType.DMA,
            pltpu.SemaphoreType.DMA,
        ],
        name="patches",
        compiler_params=pltpu.CompilerParams(vmem_limit_bytes=26 << 20),
    )(corner_rows, corner_cols, live_counts, body, state, blend_weight, above, below, from_left, from_right, w1, w2, w3))


def solution(mesh):
    placed = (
        P(None, "tile", "sub"),
        P(None, "tile", "sub"),
        P("tile", "sub", None),
        P("tile", "sub", None),
        P("tile", "sub"),
        P("tile", "sub", None, None, None),
        P(),
        P(),
        P(),
    )
    return jax.shard_map(
        per_device,
        mesh=mesh,
        in_specs=placed,
        out_specs=(P(None, "tile", "sub"), P(None, "tile", "sub")),
        check_vma=False,
    )
```

profile of v0, /device:TPU:10, one launch (start us, length us, event | category | flops | bytes accessed | tf_op | source)
XLA Modules:
  0.0 47.5 jit_solution(7658293581886618321)
XLA Ops:
  1.3 0.0 copy-start.6
  1.3 0.0 copy-start.5
  1.3 1.9 %pack_tile.1 = (bf16[208,128]{1,0:T(8,128)(2,1)}, bf16[208,128]{1,0:T(8,128)(2,1)}) custom-call(s32[1,1,2]{2,1,0:T(1,128)} %rows_ref.5, s32[1,1,2]{2,1,0:T(1,128)} %cols_ref.5, s32[1,1]{1,0:T(1,128)S(6)} %copy.18.live_ref, bf16[12,256,256]{2,1,0:T(8,128)(2,1)} %c_bot.1, bf16[12,256,256]{2,1,0:T(8,128)(2,1)} %c_bot.1, f32[4,256,256]{2,1,0:T(8,128)} %state_ref.3, ...), custom_call_target="tpu_custom_call" | custom-call | tf_op jit(solution)/shard_map/pack_tile/pallas_call | solution.py:433
  3.2 2.1 %collective-permute-start = (bf16[208,128]{1,0:T(8,128)(2,1)}, bf16[208,128]{1,0:T(8,128)(2,1)S(1)}, u32[]{:S(2)}, u32[]{:S(2)}) collective-permute-start(bf16[208,128]{1,0:T(8,128)(2,1)} %get-tuple-element.9), channel_id=1, source_target_pairs={{0,4},{4,8},{8,12},{12,16},{16,20},{20,24},{24,28},{28,32},{32,36}... | collective-permute-start | bytes 159752 | tf_op jit(solution)/shard_map/ppermute | solution.py:425
  5.3 7.1 %collective-permute-start.1 = (bf16[208,128]{1,0:T(8,128)(2,1)}, bf16[208,128]{1,0:T(8,128)(2,1)S(1)}, u32[]{:S(2)}, u32[]{:S(2)}) collective-permute-start(bf16[208,128]{1,0:T(8,128)(2,1)} %get-tuple-element.10), channel_id=1, source_target_pairs={{4,0},{8,4},{12,8},{16,12},{20,16},{24,20},{28,24},{32,28},{36,32}... | collective-permute-start | bytes 159752 | tf_op jit(solution)/shard_map/ppermute | solution.py:425
  12.4 0.1 copy.13
  12.5 0.1 copy.15
  12.7 0.1 copy.16
  12.8 0.1 fusion.2.w2_ref
  12.9 0.1 fusion.5.w1_ref
  13.0 0.0 copy-done.7
  13.0 0.0 copy-done
  13.0 0.0 copy-done.1
  13.0 2.3 %prepare.1 = (bf16[2,4096,128]{2,1,0:T(8,128)(2,1)S(1)}, bf16[16,4096]{1,0:T(8,128)(2,1)S(1)}) custom-call(bf16[12,256,256]{2,1,0:T(8,128)(2,1)S(1)} %copy-done.1, f32[4,256,256]{2,1,0:T(8,128)S(1)} %copy-done), custom_call_target="tpu_custom_call" | custom-call | flops 536870912 | bytes 5242880 | tf_op jit(solution)/shard_map/prepare/pallas_call | solution.py:455
  15.4 0.0 collective-permute-done.above_ref
  15.4 0.0 collective-permute-done.1.below_ref
  15.4 0.0 copy-done.2
  15.4 0.7 %pack_sub.1 = (bf16[400,128]{1,0:T(8,128)(2,1)S(1)}, bf16[400,128]{1,0:T(8,128)(2,1)S(1)}) custom-call(s32[1,1,2]{2,1,0:T(1,128)S(1)} %copy-done.3, s32[1,1,2]{2,1,0:T(1,128)S(1)} %copy-done.4, s32[1,1]{1,0:T(1,128)S(6)} %copy.18.live_ref, f32[1,1,2,128,128]{4,3,2,1,0:T(8,128)S(1)} %copy-done.2, bf16[16,4096]{1,0:T(8,128)(2,1)S(1)} %get-tuple-element.11.edge_ref, ...), custom_call_target="tpu_custom_call" | custom-call | tf_op jit(solution)/shard_map/pack_sub/pallas_call | solution.py:465
  16.1 3.4 %collective-permute-start.2 = (bf16[400,128]{1,0:T(8,128)(2,1)S(1)}, bf16[400,128]{1,0:T(8,128)(2,1)S(1)}, u32[]{:S(2)}, u32[]{:S(2)}) collective-permute-start(bf16[400,128]{1,0:T(8,128)(2,1)S(1)} %get-tuple-element.12), channel_id=1, source_target_pairs={{0,1},{1,2},{2,3},{4,5},{5,6},{6,7},{8,9},{9,10},{10,11},{12,13},{... | collective-permute-start | bytes 307208 | tf_op jit(solution)/shard_map/ppermute | solution.py:425
  19.5 2.4 %collective-permute-start.3 = (bf16[400,128]{1,0:T(8,128)(2,1)S(1)}, bf16[400,128]{1,0:T(8,128)(2,1)S(1)}, u32[]{:S(2)}, u32[]{:S(2)}) collective-permute-start(bf16[400,128]{1,0:T(8,128)(2,1)S(1)} %get-tuple-element.13), channel_id=1, source_target_pairs={{1,0},{2,1},{3,2},{5,4},{6,5},{7,6},{9,8},{10,9},{11,10},{13,12},{... | collective-permute-start | bytes 307208 | tf_op jit(solution)/shard_map/ppermute | solution.py:425
  22.0 0.1 fusion.13.w3_ref
  22.0 0.6 %collective-permute-done.2.left_ref = bf16[400,128]{1,0:T(8,128)(2,1)S(1)} collective-permute-done((bf16[400,128]{1,0:T(8,128)(2,1)S(1)}, bf16[400,128]{1,0:T(8,128)(2,1)S(1)}, u32[]{:S(2)}, u32[]{:S(2)}) %collective-permute-start.2) | collective-permute-done | bytes 102432 | tf_op jit(solution)/shard_map/ppermute | solution.py:425
  22.7 3.4 %collective-permute-done.3.right_ref = bf16[400,128]{1,0:T(8,128)(2,1)S(1)} collective-permute-done((bf16[400,128]{1,0:T(8,128)(2,1)S(1)}, bf16[400,128]{1,0:T(8,128)(2,1)S(1)}, u32[]{:S(2)}, u32[]{:S(2)}) %collective-permute-start.3) | collective-permute-done | bytes 102432 | tf_op jit(solution)/shard_map/ppermute | solution.py:425
  26.1 21.4 %patches.1 = (f32[4,256,256]{2,1,0:T(8,128)}, f32[4,256,256]{2,1,0:T(8,128)}) custom-call(s32[1,1,2]{2,1,0:T(1,128)S(1)} %copy-done.3, s32[1,1,2]{2,1,0:T(1,128)S(1)} %copy-done.4, s32[1,1]{1,0:T(1,128)S(6)} %copy.18.live_ref, bf16[2,4096,128]{2,1,0:T(8,128)(2,1)S(1)} %get-tuple-element.8.body_ref, f32[4,256,256]{2,1,0:T(8,128)S(1)} %copy-done, ...), custom_call_target="tpu_custom_call" | custom-call | tf_op jit(solution)/shard_map/patches/pallas_call | solution.py:476
  (13 shorter events, 0.0 us)
Async XLA Ops:
  1.3 11.1 %copy-start.6 = (bf16[3,3,64,16]{2,3,1,0:T(8,128)(2,1)S(1)}, bf16[3,3,64,16]{2,3,1,0:T(8,128)(2,1)}, u32[]{:S(2)}) copy-start(bf16[3,3,64,16]{2,3,1,0:T(8,128)(2,1)} %param.15) | copy-start | bytes 55300
  1.3 11.2 %copy-start.5 = (bf16[3,3,64,64]{3,2,1,0:T(8,128)(2,1)S(1)}, bf16[3,3,64,64]{3,2,1,0:T(8,128)(2,1)}, u32[]{:S(2)}) copy-start(bf16[3,3,64,64]{3,2,1,0:T(8,128)(2,1)} %param.16) | copy-start | bytes 221188
  1.3 11.7 %copy-start.7 = (bf16[4,64]{1,0:T(4,128)(2,1)S(1)}, bf16[4,64]{1,0:T(4,128)(2,1)}, u32[]{:S(2)}) copy-start(bf16[4,64]{1,0:T(4,128)(2,1)} %param.17) | copy-start | bytes 1540
  1.3 11.7 %copy-start = (f32[4,256,256]{2,1,0:T(8,128)S(1)}, f32[4,256,256]{2,1,0:T(8,128)}, u32[]{:S(2)}) copy-start(f32[4,256,256]{2,1,0:T(8,128)} %state_ref.3) | copy-start | bytes 3145732
  1.3 11.7 %copy-start.1 = (bf16[12,256,256]{2,1,0:T(8,128)(2,1)S(1)}, bf16[12,256,256]{2,1,0:T(8,128)(2,1)}, u32[]{:S(2)}) copy-start(bf16[12,256,256]{2,1,0:T(8,128)(2,1)} %c_bot.1) | copy-start | bytes 4718596
  3.2 12.2 %copy-start.2 = (f32[1,1,2,128,128]{4,3,2,1,0:T(8,128)S(1)}, f32[1,1,2,128,128]{4,3,2,1,0:T(8,128)}, u32[]{:S(2)}) copy-start(f32[1,1,2,128,128]{4,3,2,1,0:T(8,128)} %weight_ref.5) | copy-start | bytes 393220
  3.2 12.2 %copy-start.3 = (s32[1,1,2]{2,1,0:T(1,128)S(1)}, s32[1,1,2]{2,1,0:T(1,128)}, u32[]{:S(2)}) copy-start(s32[1,1,2]{2,1,0:T(1,128)} %rows_ref.5) | copy-start | bytes 28
  3.2 12.2 %copy-start.4 = (s32[1,1,2]{2,1,0:T(1,128)S(1)}, s32[1,1,2]{2,1,0:T(1,128)}, u32[]{:S(2)}) copy-start(s32[1,1,2]{2,1,0:T(1,128)} %cols_ref.5) | copy-start | bytes 28
  3.2 12.2 %collective-permute-start = (bf16[208,128]{1,0:T(8,128)(2,1)}, bf16[208,128]{1,0:T(8,128)(2,1)S(1)}, u32[]{:S(2)}, u32[]{:S(2)}) collective-permute-start(bf16[208,128]{1,0:T(8,128)(2,1)} %get-tuple-element.9), channel_id=1, source_target_pairs={{0,4},{4,8},{8,12},{12,16},{16,20},{20,24},{24,28},{28,32},{32,36}... | collective-permute-start | bytes 159752 | tf_op jit(solution)/shard_map/ppermute | solution.py:425
  5.3 10.1 %collective-permute-start.1 = (bf16[208,128]{1,0:T(8,128)(2,1)}, bf16[208,128]{1,0:T(8,128)(2,1)S(1)}, u32[]{:S(2)}, u32[]{:S(2)}) collective-permute-start(bf16[208,128]{1,0:T(8,128)(2,1)} %get-tuple-element.10), channel_id=1, source_target_pairs={{4,0},{8,4},{12,8},{16,12},{20,16},{24,20},{28,24},{32,28},{36,32}... | collective-permute-start | bytes 159752 | tf_op jit(solution)/shard_map/ppermute | solution.py:425
  16.1 6.6 %collective-permute-start.2 = (bf16[400,128]{1,0:T(8,128)(2,1)S(1)}, bf16[400,128]{1,0:T(8,128)(2,1)S(1)}, u32[]{:S(2)}, u32[]{:S(2)}) collective-permute-start(bf16[400,128]{1,0:T(8,128)(2,1)S(1)} %get-tuple-element.12), channel_id=1, source_target_pairs={{0,1},{1,2},{2,3},{4,5},{5,6},{6,7},{8,9},{9,10},{10,11},{12,13},{... | collective-permute-start | bytes 307208 | tf_op jit(solution)/shard_map/ppermute | solution.py:425
  19.5 6.6 %collective-permute-start.3 = (bf16[400,128]{1,0:T(8,128)(2,1)S(1)}, bf16[400,128]{1,0:T(8,128)(2,1)S(1)}, u32[]{:S(2)}, u32[]{:S(2)}) collective-permute-start(bf16[400,128]{1,0:T(8,128)(2,1)S(1)} %get-tuple-element.13), channel_id=1, source_target_pairs={{1,0},{2,1},{3,2},{5,4},{6,5},{7,6},{9,8},{10,9},{11,10},{13,12},{... | collective-permute-start | bytes 307208 | tf_op jit(solution)/shard_map/ppermute | solution.py:425
where the time goes:
time: 47 us; the launch traced here: 47.5 us
  Pallas kernels  26.3 us (56%)
  starting transfers between devices  15 us (32%)
  waiting for transfers between devices  4.03 us (9%)
  between operations  1.47 us (3%)
    pallas_call x1, Pallas kernels, per_device(): pl.pallas_call(main_kernel, in_specs=[smem] * 3 + [vmem] * 10, out_specs=...  21.4 us
    ppermute x4, starting transfers between devices, shifted(): lax.ppermute(value, axis, [(i, i + steps) for i in range(first, last)])  15 us
    ppermute x4, waiting for transfers between devices, shifted(): lax.ppermute(value, axis, [(i, i + steps) for i in range(first, last)])  4.03 us
    pallas_call x1, Pallas kernels, per_device(): pl.pallas_call(prepare, in_specs=[vmem] * 2, out_specs=[vmem] * 2, out_sh...  2.34 us
    pallas_call x1, Pallas kernels, per_device(): pl.pallas_call(pack_tile, grid=(1,), in_specs=[smem, smem, smem, pl.Block...  1.88 us
  transfers between devices with their start and end apart: 4, of which 2 were waited for; matrix products, arithmetic and copies ran while one was open for 1% of the time, Pallas kernels for 5%

commit v1 on v0

--- a/solution.py
+++ b/solution.py
@@ -52,24 +52,19 @@
     return tile
 
 
-def pack_tile(rows_ref, cols_ref, live_ref, c_top, c_bot, s_top, s_bot, weight_ref, up_ref, down_ref, tmp):
+def pack_tile(rows_ref, cols_ref, live_ref, c_top, c_bot, s_top, s_bot, weight_ref, up_ref, down_ref):
     meta = own_meta(rows_ref, cols_ref, live_ref).astype(F32).astype(BF16)
-    for out, cond, state, low, first_c, first_s in (
-        (up_ref, c_top, s_top, 0, 0, 0),
-        (down_ref, c_bot, s_bot, HALF, 14, 6),
-    ):
+    to = iota((2 * CH, CH * CH), 0)
+    of = iota((2 * CH, CH * CH), 1)
+    for out, cond, state, low, first in ((up_ref, c_top, s_top, 0, 0), (down_ref, c_bot, s_bot, HALF, CH - 2)):
         for p in range(SLOTS):
             out[p * HALF : (p + 1) * HALF, :] = weight_ref[0, 0, p, low : low + HALF, :].astype(BF16)
-        for c in range(CH):
-            if c < CC:
-                tile = cond[c].astype(F32)[first_c : first_c + 2, :]
-            else:
-                tile = scaled(state[c - CC]).astype(F32)[first_s : first_s + 2, :]
-            for t in range(2):
-                for r in range(2):
-                    at = t * 2 * CH + r * CH + c
-                    tmp[at : at + 1, :] = tile[r : r + 1, t * LANES : (t + 1) * LANES]
-        out[2 * HALF : 2 * HALF + 4 * CH, :] = tmp[...].astype(BF16)
+        pick = (of == (to % CH) * CH + to // CH + first).astype(F32).astype(BF16)
+        value = jnp.concatenate([cond[...].reshape(CC * CH, BX), scaled(state[...]).reshape(OUT * CH, BX)], axis=0)
+        value = jnp.dot(pick, value, preferred_element_type=F32).astype(BF16)
+        for t in range(2):
+            at = 2 * HALF + t * 2 * CH
+            out[at : at + 2 * CH, :] = value[:, t * LANES : (t + 1) * LANES]
         out[2 * HALF + 4 * CH :, :] = meta
 
 
@@ -139,8 +134,8 @@
 def main_kernel(
     rows_ref, cols_ref, live_ref, body_ref, state_ref, weight_ref,
     above_ref, below_ref, left_ref, right_ref, w1_ref, w2_ref, w3_ref,
-    den_ref, next_ref,
-    xb_ref, p_ref, a_ref, u_ref, q_ref, acc_ref, wall_ref, meta_v, meta_s, unit_ref, place_ref, list_ref, sem, body_sem,
+    den_out, next_out,
+    xb_ref, p_ref, a_ref, u_ref, q_ref, acc_ref, wall_ref, meta_v, meta_s, unit_ref, place_ref, list_ref, den_ref, next_ref, sem, body_sem, out_sems,
 ):
     lane = iota((1, LANES), 1)
     first = 2 * HALF + 4 * CH
@@ -382,8 +377,8 @@
     def step(i, carry):
         at, row = carry
         for z in range(2):
+            first_conv(2 * i + z + 2, z)
             blend(2 * i + z)
-            first_conv(2 * i + z + 2, z)
             second_conv(1 - z)
             stage(2 * i + z + 3, 1 - z)
         return more(i + 1, at, row)
@@ -407,9 +402,14 @@
                 den = (state * (1.0 + C_SKIP * total) + C_OUT * numer) * over
                 den_ref[o, pl.ds(row, 8), lanes] = den
                 next_ref[o, pl.ds(row, 8), lanes] = state + (SIGMA_NEXT - SIGMA) * (state - den) / SIGMA
+        rows = pl.ds(pl.multiple_of(i * 32, 32), 32)
+        for held, out, at in ((den_ref, den_out, 0), (next_ref, next_out, 1)):
+            pltpu.make_async_copy(held.at[:, rows, :], out.at[:, rows, :], out_sems.at[at]).start()
         return carry
 
     lax.fori_loop(0, BY // 32, finish, 0)
+    for held, out, at in ((den_ref, den_out, 0), (next_ref, next_out, 1)):
+        pltpu.make_async_copy(held, out, out_sems.at[at]).wait()
 
 
 def banded(kernel, times):
@@ -437,13 +437,12 @@
             smem, smem, smem,
             pl.BlockSpec((CC, 16, BX), lambda i: (0, 0, 0)),
             pl.BlockSpec((CC, 16, BX), lambda i: (0, BY // 16 - 1, 0)),
-            pl.BlockSpec((OUT, 8, BX), lambda i: (0, 0, 0)),
-            pl.BlockSpec((OUT, 8, BX), lambda i: (0, BY // 8 - 1, 0)),
+            pl.BlockSpec((OUT, 16, BX), lambda i: (0, 0, 0)),
+            pl.BlockSpec((OUT, 16, BX), lambda i: (0, BY // 16 - 1, 0)),
             whole_w,
         ],
         out_specs=[pl.BlockSpec((TILE_MSG, LANES), lambda i: (0, 0))] * 2,
         out_shape=[msg, msg],
-        scratch_shapes=[pltpu.VMEM((4 * CH, LANES), F32)],
         name="pack_tile",
     )(corner_rows, corner_cols, live_counts, condition, condition, state, state, blend_weight)
     above = shifted(down, "tile", 1)
@@ -476,7 +475,7 @@
     return tuple(pl.pallas_call(
         main_kernel,
         in_specs=[smem] * 3 + [vmem] * 10,
-        out_specs=[vmem] * 2,
+        out_specs=[pl.BlockSpec(memory_space=pl.ANY)] * 2,
         out_shape=[out, out],
         scratch_shapes=[
             pltpu.VMEM((5, X_ROWS * CH, LANES), BF16),
@@ -491,8 +490,11 @@
             pltpu.SMEM((4, UNITS), jnp.int32),
             pltpu.SMEM((11, PIECES), jnp.int32),
             pltpu.SMEM((5, LANES), jnp.int32),
+            pltpu.VMEM((OUT, BY, BX), F32),
+            pltpu.VMEM((OUT, BY, BX), F32),
             pltpu.SemaphoreType.DMA,
             pltpu.SemaphoreType.DMA,
+            pltpu.SemaphoreType.DMA((2,)),
         ],
         name="patches",
         compiler_params=pltpu.CompilerParams(vmem_limit_bytes=26 << 20),

time: 47 us -> 48.2 us (1.026)
  the two profiles are of different devices: /device:TPU:10 before, /device:TPU:20 now
where the time goes in v1:
time: 48.2 us
  Pallas kernels  27.3 us (57%)
  starting transfers between devices  15 us (31%)
  waiting for transfers between devices  3.74 us (8%)
  between operations  1.47 us (3%)
    pallas_call x1, Pallas kernels, per_device(): pl.pallas_call(main_kernel, in_specs=[smem] * 3 + [vmem] * 10, out_specs=...  22.3 us
    ppermute x4, starting transfers between devices, shifted(): lax.ppermute(value, axis, [(i, i + steps) for i in range(first, last)])  15 us
    ppermute x4, waiting for transfers between devices, shifted(): lax.ppermute(value, axis, [(i, i + steps) for i in range(first, last)])  3.74 us
    pallas_call x1, Pallas kernels, per_device(): pl.pallas_call(prepare, in_specs=[vmem] * 2, out_specs=[vmem] * 2, out_sh...  2.34 us
    pallas_call x1, Pallas kernels, per_device(): pl.pallas_call(pack_tile, grid=(1,), in_specs=[smem, smem, smem, pl.Block...  2.03 us
  transfers between devices with their start and end apart: 4, of which 2 were waited for; matrix products, arithmetic and copies ran while one was open for 1% of the time, Pallas kernels for 5%

profile of v1, /device:TPU:20, one launch (start us, length us, event | category | flops | bytes accessed | tf_op | source)
XLA Modules:
  0.0 48.2 jit_solution(5077689054109833067)
XLA Ops:
  1.3 0.0 copy-start.6
  1.3 0.0 copy-start.5
  1.3 0.0 copy-start.7
  1.3 0.0 copy-start
  1.3 0.0 copy-start.1
  1.3 2.0 %pack_tile.1 = (bf16[208,128]{1,0:T(8,128)(2,1)}, bf16[208,128]{1,0:T(8,128)(2,1)}) custom-call(s32[1,1,2]{2,1,0:T(1,128)} %rows_ref.5, s32[1,1,2]{2,1,0:T(1,128)} %cols_ref.5, s32[1,1]{1,0:T(1,128)S(6)} %copy.18.live_ref, bf16[12,256,256]{2,1,0:T(8,128)(2,1)} %c_bot.1, bf16[12,256,256]{2,1,0:T(8,128)(2,1)} %c_bot.1, f32[4,256,256]{2,1,0:T(8,128)} %state_ref.3, ...), custom_call_target="tpu_custom_call" | custom-call | tf_op jit(solution)/shard_map/pack_tile/pallas_call | solution.py:433
  3.4 2.1 %collective-permute-start = (bf16[208,128]{1,0:T(8,128)(2,1)}, bf16[208,128]{1,0:T(8,128)(2,1)S(1)}, u32[]{:S(2)}, u32[]{:S(2)}) collective-permute-start(bf16[208,128]{1,0:T(8,128)(2,1)} %get-tuple-element.9), channel_id=1, source_target_pairs={{0,4},{4,8},{8,12},{12,16},{16,20},{20,24},{24,28},{28,32},{32,36}... | collective-permute-start | bytes 159752 | tf_op jit(solution)/shard_map/ppermute | solution.py:425
  5.4 7.1 %collective-permute-start.1 = (bf16[208,128]{1,0:T(8,128)(2,1)}, bf16[208,128]{1,0:T(8,128)(2,1)S(1)}, u32[]{:S(2)}, u32[]{:S(2)}) collective-permute-start(bf16[208,128]{1,0:T(8,128)(2,1)} %get-tuple-element.10), channel_id=1, source_target_pairs={{4,0},{8,4},{12,8},{16,12},{20,16},{24,20},{28,24},{32,28},{36,32}... | collective-permute-start | bytes 159752 | tf_op jit(solution)/shard_map/ppermute | solution.py:425
  12.5 0.1 copy.13
  12.7 0.1 copy.15
  12.8 0.1 copy.16
  13.0 0.1 fusion.2.w2_ref
  13.1 0.1 fusion.5.w1_ref
  13.2 2.3 %prepare.1 = (bf16[2,4096,128]{2,1,0:T(8,128)(2,1)S(1)}, bf16[16,4096]{1,0:T(8,128)(2,1)S(1)}) custom-call(bf16[12,256,256]{2,1,0:T(8,128)(2,1)S(1)} %copy-done.1, f32[4,256,256]{2,1,0:T(8,128)S(1)} %copy-done), custom_call_target="tpu_custom_call" | custom-call | flops 536870912 | bytes 5242880 | tf_op jit(solution)/shard_map/prepare/pallas_call | solution.py:454
  15.5 0.0 collective-permute-done.above_ref
  15.5 0.0 collective-permute-done.1.below_ref
  15.6 0.0 copy-done.2
  15.6 0.7 %pack_sub.1 = (bf16[400,128]{1,0:T(8,128)(2,1)S(1)}, bf16[400,128]{1,0:T(8,128)(2,1)S(1)}) custom-call(s32[1,1,2]{2,1,0:T(1,128)S(1)} %copy-done.3, s32[1,1,2]{2,1,0:T(1,128)S(1)} %copy-done.4, s32[1,1]{1,0:T(1,128)S(6)} %copy.18.live_ref, f32[1,1,2,128,128]{4,3,2,1,0:T(8,128)S(1)} %copy-done.2, bf16[16,4096]{1,0:T(8,128)(2,1)S(1)} %get-tuple-element.11.edge_ref, ...), custom_call_target="tpu_custom_call" | custom-call | tf_op jit(solution)/shard_map/pack_sub/pallas_call | solution.py:464
  16.2 3.1 %collective-permute-start.2 = (bf16[400,128]{1,0:T(8,128)(2,1)S(1)}, bf16[400,128]{1,0:T(8,128)(2,1)S(1)}, u32[]{:S(2)}, u32[]{:S(2)}) collective-permute-start(bf16[400,128]{1,0:T(8,128)(2,1)S(1)} %get-tuple-element.12), channel_id=1, source_target_pairs={{0,1},{1,2},{2,3},{4,5},{5,6},{6,7},{8,9},{9,10},{10,11},{12,13},{... | collective-permute-start | bytes 307208 | tf_op jit(solution)/shard_map/ppermute | solution.py:425
  19.4 2.7 %collective-permute-start.3 = (bf16[400,128]{1,0:T(8,128)(2,1)S(1)}, bf16[400,128]{1,0:T(8,128)(2,1)S(1)}, u32[]{:S(2)}, u32[]{:S(2)}) collective-permute-start(bf16[400,128]{1,0:T(8,128)(2,1)S(1)} %get-tuple-element.13), channel_id=1, source_target_pairs={{1,0},{2,1},{3,2},{5,4},{6,5},{7,6},{9,8},{10,9},{11,10},{13,12},{... | collective-permute-start | bytes 307208 | tf_op jit(solution)/shard_map/ppermute | solution.py:425
  22.1 0.1 fusion.13.w3_ref
  22.2 0.6 %collective-permute-done.2.left_ref = bf16[400,128]{1,0:T(8,128)(2,1)S(1)} collective-permute-done((bf16[400,128]{1,0:T(8,128)(2,1)S(1)}, bf16[400,128]{1,0:T(8,128)(2,1)S(1)}, u32[]{:S(2)}, u32[]{:S(2)}) %collective-permute-start.2) | collective-permute-done | bytes 102432 | tf_op jit(solution)/shard_map/ppermute | solution.py:425
  22.8 3.1 %collective-permute-done.3.right_ref = bf16[400,128]{1,0:T(8,128)(2,1)S(1)} collective-permute-done((bf16[400,128]{1,0:T(8,128)(2,1)S(1)}, bf16[400,128]{1,0:T(8,128)(2,1)S(1)}, u32[]{:S(2)}, u32[]{:S(2)}) %collective-permute-start.3) | collective-permute-done | bytes 102432 | tf_op jit(solution)/shard_map/ppermute | solution.py:425
  25.9 22.3 %patches.1 = (f32[4,256,256]{2,1,0:T(8,128)}, f32[4,256,256]{2,1,0:T(8,128)}) custom-call(s32[1,1,2]{2,1,0:T(1,128)S(1)} %copy-done.3, s32[1,1,2]{2,1,0:T(1,128)S(1)} %copy-done.4, s32[1,1]{1,0:T(1,128)S(6)} %copy.18.live_ref, bf16[2,4096,128]{2,1,0:T(8,128)(2,1)S(1)} %get-tuple-element.8.body_ref, f32[4,256,256]{2,1,0:T(8,128)S(1)} %copy-done, ...), custom_call_target="tpu_custom_call" | custom-call | tf_op jit(solution)/shard_map/patches/pallas_call | solution.py:475
  (13 shorter events, 0.0 us)
Async XLA Ops:
  1.3 11.2 %copy-start.6 = (bf16[3,3,64,16]{2,3,1,0:T(8,128)(2,1)S(1)}, bf16[3,3,64,16]{2,3,1,0:T(8,128)(2,1)}, u32[]{:S(2)}) copy-start(bf16[3,3,64,16]{2,3,1,0:T(8,128)(2,1)} %param.15) | copy-start | bytes 55300
  1.3 11.4 %copy-start.5 = (bf16[3,3,64,64]{3,2,1,0:T(8,128)(2,1)S(1)}, bf16[3,3,64,64]{3,2,1,0:T(8,128)(2,1)}, u32[]{:S(2)}) copy-start(bf16[3,3,64,64]{3,2,1,0:T(8,128)(2,1)} %param.16) | copy-start | bytes 221188
  1.3 11.9 %copy-start.7 = (bf16[4,64]{1,0:T(4,128)(2,1)S(1)}, bf16[4,64]{1,0:T(4,128)(2,1)}, u32[]{:S(2)}) copy-start(bf16[4,64]{1,0:T(4,128)(2,1)} %param.17) | copy-start | bytes 1540
  1.3 11.9 %copy-start = (f32[4,256,256]{2,1,0:T(8,128)S(1)}, f32[4,256,256]{2,1,0:T(8,128)}, u32[]{:S(2)}) copy-start(f32[4,256,256]{2,1,0:T(8,128)} %state_ref.3) | copy-start | bytes 3145732
  1.3 11.9 %copy-start.1 = (bf16[12,256,256]{2,1,0:T(8,128)(2,1)S(1)}, bf16[12,256,256]{2,1,0:T(8,128)(2,1)}, u32[]{:S(2)}) copy-start(bf16[12,256,256]{2,1,0:T(8,128)(2,1)} %c_bot.1) | copy-start | bytes 4718596
  3.4 12.2 %copy-start.2 = (f32[1,1,2,128,128]{4,3,2,1,0:T(8,128)S(1)}, f32[1,1,2,128,128]{4,3,2,1,0:T(8,128)}, u32[]{:S(2)}) copy-start(f32[1,1,2,128,128]{4,3,2,1,0:T(8,128)} %weight_ref.5) | copy-start | bytes 393220
  3.4 12.2 %copy-start.3 = (s32[1,1,2]{2,1,0:T(1,128)S(1)}, s32[1,1,2]{2,1,0:T(1,128)}, u32[]{:S(2)}) copy-start(s32[1,1,2]{2,1,0:T(1,128)} %rows_ref.5) | copy-start | bytes 28
  3.4 12.2 %copy-start.4 = (s32[1,1,2]{2,1,0:T(1,128)S(1)}, s32[1,1,2]{2,1,0:T(1,128)}, u32[]{:S(2)}) copy-start(s32[1,1,2]{2,1,0:T(1,128)} %cols_ref.5) | copy-start | bytes 28
  3.4 12.2 %collective-permute-start = (bf16[208,128]{1,0:T(8,128)(2,1)}, bf16[208,128]{1,0:T(8,128)(2,1)S(1)}, u32[]{:S(2)}, u32[]{:S(2)}) collective-permute-start(bf16[208,128]{1,0:T(8,128)(2,1)} %get-tuple-element.9), channel_id=1, source_target_pairs={{0,4},{4,8},{8,12},{12,16},{16,20},{20,24},{24,28},{28,32},{32,36}... | collective-permute-start | bytes 159752 | tf_op jit(solution)/shard_map/ppermute | solution.py:425
  5.4 10.1 %collective-permute-start.1 = (bf16[208,128]{1,0:T(8,128)(2,1)}, bf16[208,128]{1,0:T(8,128)(2,1)S(1)}, u32[]{:S(2)}, u32[]{:S(2)}) collective-permute-start(bf16[208,128]{1,0:T(8,128)(2,1)} %get-tuple-element.10), channel_id=1, source_target_pairs={{4,0},{8,4},{12,8},{16,12},{20,16},{24,20},{28,24},{32,28},{36,32}... | collective-permute-start | bytes 159752 | tf_op jit(solution)/shard_map/ppermute | solution.py:425
  16.2 6.6 %collective-permute-start.2 = (bf16[400,128]{1,0:T(8,128)(2,1)S(1)}, bf16[400,128]{1,0:T(8,128)(2,1)S(1)}, u32[]{:S(2)}, u32[]{:S(2)}) collective-permute-start(bf16[400,128]{1,0:T(8,128)(2,1)S(1)} %get-tuple-element.12), channel_id=1, source_target_pairs={{0,1},{1,2},{2,3},{4,5},{5,6},{6,7},{8,9},{9,10},{10,11},{12,13},{... | collective-permute-start | bytes 307208 | tf_op jit(solution)/shard_map/ppermute | solution.py:425
  19.4 6.6 %collective-permute-start.3 = (bf16[400,128]{1,0:T(8,128)(2,1)S(1)}, bf16[400,128]{1,0:T(8,128)(2,1)S(1)}, u32[]{:S(2)}, u32[]{:S(2)}) collective-permute-start(bf16[400,128]{1,0:T(8,128)(2,1)S(1)} %get-tuple-element.13), channel_id=1, source_target_pairs={{1,0},{2,1},{3,2},{5,4},{6,5},{7,6},{9,8},{10,9},{11,10},{13,12},{... | collective-permute-start | bytes 307208 | tf_op jit(solution)/shard_map/ppermute | solution.py:425

commit v2 on v0

--- a/solution.py
+++ b/solution.py
@@ -139,8 +139,8 @@
 def main_kernel(
     rows_ref, cols_ref, live_ref, body_ref, state_ref, weight_ref,
     above_ref, below_ref, left_ref, right_ref, w1_ref, w2_ref, w3_ref,
-    den_ref, next_ref,
-    xb_ref, p_ref, a_ref, u_ref, q_ref, acc_ref, wall_ref, meta_v, meta_s, unit_ref, place_ref, list_ref, sem, body_sem,
+    den_out, next_out,
+    xb_ref, p_ref, a_ref, u_ref, q_ref, acc_ref, wall_ref, meta_v, meta_s, unit_ref, place_ref, list_ref, den_ref, next_ref, sem, body_sem, out_sems,
 ):
     lane = iota((1, LANES), 1)
     first = 2 * HALF + 4 * CH
@@ -305,9 +305,9 @@
         for m in range(part.shape[0] // CH):
             ref[z, row + m * CH : row + (m + 1) * CH, h * LANES : (h + 1) * LANES] = jnp.where(mask > 0, part[m * CH : (m + 1) * CH], jnp.zeros((), BF16))
 
-    def blend(i):
+    def blend(i, z):
         nets = [
-            jnp.dot(w3_ref[...], q_ref[4 * e * HID : 4 * (e + 1) * HID, :], preferred_element_type=F32)
+            jnp.dot(w3_ref[...], q_ref[z, 4 * e * HID : 4 * (e + 1) * HID, :], preferred_element_type=F32)
             for e in range(STEP // 4)
         ]
         for h in range(2):
@@ -326,11 +326,11 @@
                 at = pl.ds(pl.multiple_of((unit_ref[2, units[g]] + STEP) * 8, 8), 8 * STEP)
                 acc_ref[tile, at, :] += jnp.where((lane >= lo) & (lane < hi), y, 0.0)
 
-    def second_conv(z):
+    def second_conv(z, y):
         for e in range(STEP // 2):
             v = jnp.dot(w2_ref[...], a_ref[z, 2 * e * 3 * HID : (2 * e + 4) * 3 * HID, :], preferred_element_type=F32)
             v = v + u_ref[z, (2 * e + 1) * HID : (2 * e + 3) * HID, :]
-            q_ref[2 * e * HID : (2 * e + 2) * HID, :] = (v + v * jnp.tanh(v)).astype(BF16)
+            q_ref[y, 2 * e * HID : (2 * e + 2) * HID, :] = (v + v * jnp.tanh(v)).astype(BF16)
 
     def first_conv(i, z):
         for e in range(STEP // 2 + 1):
@@ -382,9 +382,9 @@
     def step(i, carry):
         at, row = carry
         for z in range(2):
-            blend(2 * i + z)
             first_conv(2 * i + z + 2, z)
-            second_conv(1 - z)
+            blend(2 * i + z, 1 - z)
+            second_conv(1 - z, z)
             stage(2 * i + z + 3, 1 - z)
         return more(i + 1, at, row)
 
@@ -407,9 +407,14 @@
                 den = (state * (1.0 + C_SKIP * total) + C_OUT * numer) * over
                 den_ref[o, pl.ds(row, 8), lanes] = den
                 next_ref[o, pl.ds(row, 8), lanes] = state + (SIGMA_NEXT - SIGMA) * (state - den) / SIGMA
+        rows = pl.ds(pl.multiple_of(i * 32, 32), 32)
+        for held, out, at in ((den_ref, den_out, 0), (next_ref, next_out, 1)):
+            pltpu.make_async_copy(held.at[:, rows, :], out.at[:, rows, :], out_sems.at[at]).start()
         return carry
 
     lax.fori_loop(0, BY // 32, finish, 0)
+    for held, out, at in ((den_ref, den_out, 0), (next_ref, next_out, 1)):
+        pltpu.make_async_copy(held, out, out_sems.at[at]).wait()
 
 
 def banded(kernel, times):
@@ -476,14 +481,14 @@
     return tuple(pl.pallas_call(
         main_kernel,
         in_specs=[smem] * 3 + [vmem] * 10,
-        out_specs=[vmem] * 2,
+        out_specs=[pl.BlockSpec(memory_space=pl.ANY)] * 2,
         out_shape=[out, out],
         scratch_shapes=[
             pltpu.VMEM((5, X_ROWS * CH, LANES), BF16),
             pltpu.VMEM((2, (STEP + 4) * 3 * CH, WIDE), BF16),
             pltpu.VMEM((2, (STEP + 2) * 3 * HID, WIDE), BF16),
             pltpu.VMEM((2, (STEP + 2) * HID, WIDE), F32),
-            pltpu.VMEM((STEP * HID, WIDE), BF16),
+            pltpu.VMEM((2, STEP * HID, WIDE), BF16),
             pltpu.VMEM((3, ACC_ROWS * 8, LANES), F32),
             pltpu.VMEM((PIECES, SIDE, LANES), F32),
             pltpu.VMEM((80, LANES), jnp.int32),
@@ -491,8 +496,11 @@
             pltpu.SMEM((4, UNITS), jnp.int32),
             pltpu.SMEM((11, PIECES), jnp.int32),
             pltpu.SMEM((5, LANES), jnp.int32),
+            pltpu.VMEM((OUT, BY, BX), F32),
+            pltpu.VMEM((OUT, BY, BX), F32),
             pltpu.SemaphoreType.DMA,
             pltpu.SemaphoreType.DMA,
+            pltpu.SemaphoreType.DMA((2,)),
         ],
         name="patches",
         compiler_params=pltpu.CompilerParams(vmem_limit_bytes=26 << 20),

time: 47 us -> 47.8 us (1.017)
  the two profiles are of different devices: /device:TPU:10 before, /device:TPU:115 now
where the time goes in v2:
time: 47.8 us; the launch traced here: 48.2 us
  Pallas kernels  28.3 us (59%)
  starting transfers between devices  12.7 us (27%)
  waiting for transfers between devices  5.09 us (11%)
  between operations  1.43 us (3%)
    pallas_call x1, Pallas kernels, per_device(): pl.pallas_call(main_kernel, in_specs=[smem] * 3 + [vmem] * 10, out_specs=...  23.4 us
    ppermute x4, starting transfers between devices, shifted(): lax.ppermute(value, axis, [(i, i + steps) for i in range(first, last)])  12.7 us
    ppermute x4, waiting for transfers between devices, shifted(): lax.ppermute(value, axis, [(i, i + steps) for i in range(first, last)])  5.09 us
    pallas_call x1, Pallas kernels, per_device(): pl.pallas_call(prepare, in_specs=[vmem] * 2, out_specs=[vmem] * 2, out_sh...  2.34 us
    pallas_call x1, Pallas kernels, per_device(): pl.pallas_call(pack_tile, grid=(1,), in_specs=[smem, smem, smem, pl.Block...  1.88 us
  transfers between devices with their start and end apart: 4, of which 3 were waited for; matrix products, arithmetic and copies ran while one was open for 1% of the time, Pallas kernels for 5%

profile of v2, /device:TPU:115, one launch (start us, length us, event | category | flops | bytes accessed | tf_op | source)
XLA Modules:
  0.0 48.2 jit_solution(6594941199533218325)
XLA Ops:
  1.3 0.0 copy-start.6
  1.3 0.0 copy-start.5
  1.3 0.0 copy-start.7
  1.3 0.0 copy-start
  1.3 0.0 copy-start.1
  1.3 1.9 %pack_tile.1 = (bf16[208,128]{1,0:T(8,128)(2,1)}, bf16[208,128]{1,0:T(8,128)(2,1)}) custom-call(s32[1,1,2]{2,1,0:T(1,128)} %rows_ref.5, s32[1,1,2]{2,1,0:T(1,128)} %cols_ref.5, s32[1,1]{1,0:T(1,128)S(6)} %copy.18.live_ref, bf16[12,256,256]{2,1,0:T(8,128)(2,1)} %c_bot.1, bf16[12,256,256]{2,1,0:T(8,128)(2,1)} %c_bot.1, f32[4,256,256]{2,1,0:T(8,128)} %state_ref.3, ...), custom_call_target="tpu_custom_call" | custom-call | tf_op jit(solution)/shard_map/pack_tile/pallas_call | solution.py:438
  3.2 5.4 %collective-permute-start = (bf16[208,128]{1,0:T(8,128)(2,1)}, bf16[208,128]{1,0:T(8,128)(2,1)S(1)}, u32[]{:S(2)}, u32[]{:S(2)}) collective-permute-start(bf16[208,128]{1,0:T(8,128)(2,1)} %get-tuple-element.9), channel_id=1, source_target_pairs={{0,4},{4,8},{8,12},{12,16},{16,20},{20,24},{24,28},{28,32},{32,36}... | collective-permute-start | bytes 159752 | tf_op jit(solution)/shard_map/ppermute | solution.py:430
  8.7 1.9 %collective-permute-start.1 = (bf16[208,128]{1,0:T(8,128)(2,1)}, bf16[208,128]{1,0:T(8,128)(2,1)S(1)}, u32[]{:S(2)}, u32[]{:S(2)}) collective-permute-start(bf16[208,128]{1,0:T(8,128)(2,1)} %get-tuple-element.10), channel_id=1, source_target_pairs={{4,0},{8,4},{12,8},{16,12},{20,16},{24,20},{28,24},{32,28},{36,32}... | collective-permute-start | bytes 159752 | tf_op jit(solution)/shard_map/ppermute | solution.py:430
  10.6 0.0 copy-done.6
  10.6 0.1 copy.13
  10.8 0.1 copy.15
  10.9 0.1 copy.16
  11.1 0.1 fusion.2.w2_ref
  11.2 0.1 fusion.5.w1_ref
  11.3 2.3 %prepare.1 = (bf16[2,4096,128]{2,1,0:T(8,128)(2,1)S(1)}, bf16[16,4096]{1,0:T(8,128)(2,1)S(1)}) custom-call(bf16[12,256,256]{2,1,0:T(8,128)(2,1)S(1)} %copy-done.1, f32[4,256,256]{2,1,0:T(8,128)S(1)} %copy-done), custom_call_target="tpu_custom_call" | custom-call | flops 536870912 | bytes 5242880 | tf_op jit(solution)/shard_map/prepare/pallas_call | solution.py:460
  13.6 0.0 collective-permute-done.above_ref
  13.6 1.9 %collective-permute-done.1.below_ref = bf16[208,128]{1,0:T(8,128)(2,1)S(1)} collective-permute-done((bf16[208,128]{1,0:T(8,128)(2,1)}, bf16[208,128]{1,0:T(8,128)(2,1)S(1)}, u32[]{:S(2)}, u32[]{:S(2)}) %collective-permute-start.1) | collective-permute-done | bytes 53280 | tf_op jit(solution)/shard_map/ppermute | solution.py:430
  15.6 0.7 %pack_sub.1 = (bf16[400,128]{1,0:T(8,128)(2,1)S(1)}, bf16[400,128]{1,0:T(8,128)(2,1)S(1)}) custom-call(s32[1,1,2]{2,1,0:T(1,128)S(1)} %copy-done.3, s32[1,1,2]{2,1,0:T(1,128)S(1)} %copy-done.4, s32[1,1]{1,0:T(1,128)S(6)} %copy.18.live_ref, f32[1,1,2,128,128]{4,3,2,1,0:T(8,128)S(1)} %copy-done.2, bf16[16,4096]{1,0:T(8,128)(2,1)S(1)} %get-tuple-element.11.edge_ref, ...), custom_call_target="tpu_custom_call" | custom-call | tf_op jit(solution)/shard_map/pack_sub/pallas_call | solution.py:470
  16.2 3.1 %collective-permute-start.2 = (bf16[400,128]{1,0:T(8,128)(2,1)S(1)}, bf16[400,128]{1,0:T(8,128)(2,1)S(1)}, u32[]{:S(2)}, u32[]{:S(2)}) collective-permute-start(bf16[400,128]{1,0:T(8,128)(2,1)S(1)} %get-tuple-element.12), channel_id=1, source_target_pairs={{0,1},{1,2},{2,3},{4,5},{5,6},{6,7},{8,9},{9,10},{10,11},{12,13},{... | collective-permute-start | bytes 307208 | tf_op jit(solution)/shard_map/ppermute | solution.py:430
  19.3 2.2 %collective-permute-start.3 = (bf16[400,128]{1,0:T(8,128)(2,1)S(1)}, bf16[400,128]{1,0:T(8,128)(2,1)S(1)}, u32[]{:S(2)}, u32[]{:S(2)}) collective-permute-start(bf16[400,128]{1,0:T(8,128)(2,1)S(1)} %get-tuple-element.13), channel_id=1, source_target_pairs={{1,0},{2,1},{3,2},{5,4},{6,5},{7,6},{9,8},{10,9},{11,10},{13,12},{... | collective-permute-start | bytes 307208 | tf_op jit(solution)/shard_map/ppermute | solution.py:430
  21.5 0.1 fusion.13.w3_ref
  21.6 0.3 collective-permute-done.2.left_ref
  21.9 2.8 %collective-permute-done.3.right_ref = bf16[400,128]{1,0:T(8,128)(2,1)S(1)} collective-permute-done((bf16[400,128]{1,0:T(8,128)(2,1)S(1)}, bf16[400,128]{1,0:T(8,128)(2,1)S(1)}, u32[]{:S(2)}, u32[]{:S(2)}) %collective-permute-start.3) | collective-permute-done | bytes 102432 | tf_op jit(solution)/shard_map/ppermute | solution.py:430
  24.8 23.4 %patches.1 = (f32[4,256,256]{2,1,0:T(8,128)}, f32[4,256,256]{2,1,0:T(8,128)}) custom-call(s32[1,1,2]{2,1,0:T(1,128)S(1)} %copy-done.3, s32[1,1,2]{2,1,0:T(1,128)S(1)} %copy-done.4, s32[1,1]{1,0:T(1,128)S(6)} %copy.18.live_ref, bf16[2,4096,128]{2,1,0:T(8,128)(2,1)S(1)} %get-tuple-element.8.body_ref, f32[4,256,256]{2,1,0:T(8,128)S(1)} %copy-done, ...), custom_call_target="tpu_custom_call" | custom-call | tf_op jit(solution)/shard_map/patches/pallas_call | solution.py:481
  (13 shorter events, 0.0 us)
Async XLA Ops:
  1.3 9.3 %copy-start.6 = (bf16[3,3,64,16]{2,3,1,0:T(8,128)(2,1)S(1)}, bf16[3,3,64,16]{2,3,1,0:T(8,128)(2,1)}, u32[]{:S(2)}) copy-start(bf16[3,3,64,16]{2,3,1,0:T(8,128)(2,1)} %param.15) | copy-start | bytes 55300
  1.3 9.4 %copy-start.5 = (bf16[3,3,64,64]{3,2,1,0:T(8,128)(2,1)S(1)}, bf16[3,3,64,64]{3,2,1,0:T(8,128)(2,1)}, u32[]{:S(2)}) copy-start(bf16[3,3,64,64]{3,2,1,0:T(8,128)(2,1)} %param.16) | copy-start | bytes 221188
  1.3 9.9 %copy-start.7 = (bf16[4,64]{1,0:T(4,128)(2,1)S(1)}, bf16[4,64]{1,0:T(4,128)(2,1)}, u32[]{:S(2)}) copy-start(bf16[4,64]{1,0:T(4,128)(2,1)} %param.17) | copy-start | bytes 1540
  1.3 9.9 %copy-start = (f32[4,256,256]{2,1,0:T(8,128)S(1)}, f32[4,256,256]{2,1,0:T(8,128)}, u32[]{:S(2)}) copy-start(f32[4,256,256]{2,1,0:T(8,128)} %state_ref.3) | copy-start | bytes 3145732
  1.3 9.9 %copy-start.1 = (bf16[12,256,256]{2,1,0:T(8,128)(2,1)S(1)}, bf16[12,256,256]{2,1,0:T(8,128)(2,1)}, u32[]{:S(2)}) copy-start(bf16[12,256,256]{2,1,0:T(8,128)(2,1)} %c_bot.1) | copy-start | bytes 4718596
  3.2 12.3 %copy-start.2 = (f32[1,1,2,128,128]{4,3,2,1,0:T(8,128)S(1)}, f32[1,1,2,128,128]{4,3,2,1,0:T(8,128)}, u32[]{:S(2)}) copy-start(f32[1,1,2,128,128]{4,3,2,1,0:T(8,128)} %weight_ref.5) | copy-start | bytes 393220
  3.2 12.3 %copy-start.3 = (s32[1,1,2]{2,1,0:T(1,128)S(1)}, s32[1,1,2]{2,1,0:T(1,128)}, u32[]{:S(2)}) copy-start(s32[1,1,2]{2,1,0:T(1,128)} %rows_ref.5) | copy-start | bytes 28
  3.2 12.3 %copy-start.4 = (s32[1,1,2]{2,1,0:T(1,128)S(1)}, s32[1,1,2]{2,1,0:T(1,128)}, u32[]{:S(2)}) copy-start(s32[1,1,2]{2,1,0:T(1,128)} %cols_ref.5) | copy-start | bytes 28
  3.2 10.4 %collective-permute-start = (bf16[208,128]{1,0:T(8,128)(2,1)}, bf16[208,128]{1,0:T(8,128)(2,1)S(1)}, u32[]{:S(2)}, u32[]{:S(2)}) collective-permute-start(bf16[208,128]{1,0:T(8,128)(2,1)} %get-tuple-element.9), channel_id=1, source_target_pairs={{0,4},{4,8},{8,12},{12,16},{16,20},{20,24},{24,28},{28,32},{32,36}... | collective-permute-start | bytes 159752 | tf_op jit(solution)/shard_map/ppermute | solution.py:430
  8.7 6.9 %collective-permute-start.1 = (bf16[208,128]{1,0:T(8,128)(2,1)}, bf16[208,128]{1,0:T(8,128)(2,1)S(1)}, u32[]{:S(2)}, u32[]{:S(2)}) collective-permute-start(bf16[208,128]{1,0:T(8,128)(2,1)} %get-tuple-element.10), channel_id=1, source_target_pairs={{4,0},{8,4},{12,8},{16,12},{20,16},{24,20},{28,24},{32,28},{36,32}... | collective-permute-start | bytes 159752 | tf_op jit(solution)/shard_map/ppermute | solution.py:430
  16.2 5.7 %collective-permute-start.2 = (bf16[400,128]{1,0:T(8,128)(2,1)S(1)}, bf16[400,128]{1,0:T(8,128)(2,1)S(1)}, u32[]{:S(2)}, u32[]{:S(2)}) collective-permute-start(bf16[400,128]{1,0:T(8,128)(2,1)S(1)} %get-tuple-element.12), channel_id=1, source_target_pairs={{0,1},{1,2},{2,3},{4,5},{5,6},{6,7},{8,9},{9,10},{10,11},{12,13},{... | collective-permute-start | bytes 307208 | tf_op jit(solution)/shard_map/ppermute | solution.py:430
  19.3 5.4 %collective-permute-start.3 = (bf16[400,128]{1,0:T(8,128)(2,1)S(1)}, bf16[400,128]{1,0:T(8,128)(2,1)S(1)}, u32[]{:S(2)}, u32[]{:S(2)}) collective-permute-start(bf16[400,128]{1,0:T(8,128)(2,1)S(1)} %get-tuple-element.13), channel_id=1, source_target_pairs={{1,0},{2,1},{3,2},{5,4},{6,5},{7,6},{9,8},{10,9},{11,10},{13,12},{... | collective-permute-start | bytes 307208 | tf_op jit(solution)/shard_map/ppermute | solution.py:430
